TPU v7x, 128 devices: a whole 4x4x4 slice. The times are simulated.
128 devices in a mesh: group: 8 (over x, core), dom: 16 (over y, z).
Axes of the slice: x: 4, y: 4, z: 4, core: 2. Of those that a mesh axis runs over, the one named last changes fastest.
Arguments:
- features: bfloat16 [65536, 512], P(('group', 'dom')), may hold values from -6 to 6
- w_query: bfloat16 [512, 512], replicated
- w_key: bfloat16 [512, 512], replicated
- w_value: bfloat16 [512, 512], replicated, may hold values from -0.25 to 0.25
- w_out: bfloat16 [512, 512], replicated, may hold values from -0.25 to 0.25
- w_up: bfloat16 [512, 2048], replicated, may hold values from -0.25 to 0.25
- w_down: bfloat16 [2048, 512], replicated, may hold values from -0.125 to 0.125
- block_len: int32 [512], P(('group', 'dom')), may hold values from 32 to 128, as said below
- cross_blocks: int32 [512, 2], P(('group', 'dom')), may hold values from 0 to 511, as said below
- cross_count: int32 [512], P(('group', 'dom')), may hold values from 1 to 2, as said below
Outputs:
- layer_out: bfloat16 [65536, 512], P(('group', 'dom'))
Inputs may be any that keep to these rules, and one draw needn't show every extreme that they name: `block_len`: block 0 has all 128 nodes live. Block cross_blocks[b, c] lies in a group other than b's, at the same index of dom as block b, that is cross_blocks[b, c] // 4 % 16 == b // 4 % 16. `cross_count`: block 0 uses all 2 listed key blocks.
All inputs are finite; a program needn't handle non-finite values.
Results may differ from a plain program's by a relative error of at most 0.012.
The roundings to bfloat16 on the way count: a program that leaves them out, or rounds other values in their place, can miss the bound.
Values may be sent and summed in bfloat16 or wider, within the bound.
A program may use at most 320 MiB of HBM per device.

v0:
```python
import math

import jax
import jax.numpy as jnp
from jax import lax
from jax.sharding import PartitionSpec as P

HEADS = 8
CROSS = 2


def in_one_piece(arrays, axis, dim, along):
    widths = [math.prod(a.shape[along:]) for a in arrays]
    both = jnp.concatenate(
        [a.reshape(*a.shape[:along], w) for a, w in zip(arrays, widths)], axis=along
    )
    whole = lax.all_gather(both, axis, axis=dim, tiled=True)
    tiles = jnp.split(whole, [sum(widths[:k]) for k in range(1, len(widths))], axis=along)
    return tuple((b.reshape(*whole.shape[:along], *a.shape[along:]) for a, b in zip(arrays, tiles)))


def rms_normed(values):
    wide = values.astype(jnp.float32)
    return (wide * lax.rsqrt(jnp.mean(wide * wide, axis=-1, keepdims=True) + 1e-06)).astype(
        jnp.bfloat16
    )


def project(rows, weight):
    return jnp.dot(rows, weight, preferred_element_type=jnp.float32).astype(jnp.bfloat16)


def intra_branch(query, normed, live_flag, w_key, w_value):
    count_q = query.shape[0]
    q_heads = query.reshape(count_q, HEADS, -1)
    head_size = q_heads.shape[-1]
    scale = 1.0 / head_size**0.5
    piece = in_one_piece((normed, live_flag), "dom", 0, 1)
    k_rows = project(piece[0], w_key)
    top = jnp.full((HEADS, count_q), -1e30, jnp.float32)
    count_k = k_rows.shape[0]
    k_heads = k_rows.reshape(count_k, HEADS, head_size)
    v_heads = project(piece[0], w_value).reshape(count_k, HEADS, head_size)
    mask = (piece[1].astype(jnp.float32) > 0.5)[None, None, :]
    scores = (
        jnp.einsum("rhd,shd->hrs", q_heads, k_heads, preferred_element_type=jnp.float32) * scale
    )
    scores = jnp.where(mask, scores, -1e30)
    top_new = jnp.maximum(top, jnp.max(scores, axis=-1))
    weights = jnp.where(mask, jnp.exp(scores - top_new[:, :, None]), 0.0)
    total_new = jnp.sum(weights, axis=-1)
    added = jnp.einsum(
        "hrs,shd->rhd", weights.astype(jnp.bfloat16), v_heads, preferred_element_type=jnp.float32
    )
    return (added / jnp.transpose(total_new)[:, :, None]).reshape(count_q, -1)


def cross_branch(query, normed, live_flag, w_key, w_value, cross_blocks, cross_count):
    count_q = query.shape[0]
    blocks_here = cross_count.shape[0]
    block_rows = count_q // blocks_here
    normed_all, flag_all = (
        lax.all_gather(normed, "group", axis=0, tiled=True),
        lax.all_gather(live_flag, "group", axis=0, tiled=True),
    )
    key_all = project(normed_all, w_key)
    value_all = project(normed_all, w_value)
    per_group = lax.axis_size("dom") * blocks_here
    chosen = cross_blocks // per_group * blocks_here + cross_blocks % blocks_here
    width = query.shape[1]
    head_size = width // HEADS
    k_sel = key_all.reshape(-1, block_rows, width)[chosen].reshape(
        blocks_here, CROSS * block_rows, HEADS, head_size
    )
    v_sel = value_all.reshape(-1, block_rows, width)[chosen].reshape(
        blocks_here, CROSS * block_rows, HEADS, head_size
    )
    flags = flag_all.reshape(-1, block_rows)[chosen].astype(jnp.float32) > 0.5
    used = jnp.arange(CROSS, dtype=jnp.int32)[None, :, None] < cross_count[:, None, None]
    mask = (flags & used).reshape(blocks_here, 1, 1, CROSS * block_rows)
    q_blocks = query.reshape(blocks_here, block_rows, HEADS, head_size)
    scale = 1.0 / head_size**0.5
    scores = (
        jnp.einsum("bqhd,bshd->bhqs", q_blocks, k_sel, preferred_element_type=jnp.float32) * scale
    )
    scores = jnp.where(mask, scores, -1e30)
    top = jnp.max(scores, axis=-1, keepdims=True)
    weights = jnp.where(mask, jnp.exp(scores - top), 0.0)
    total = jnp.sum(weights, axis=-1)
    summed = jnp.einsum(
        "bhqs,bshd->bqhd", weights.astype(jnp.bfloat16), v_sel, preferred_element_type=jnp.float32
    )
    return (summed / jnp.transpose(total, (0, 2, 1))[:, :, :, None]).reshape(count_q, -1)


def body(
    features, w_query, w_key, w_value, w_out, w_up, w_down, block_len, cross_blocks, cross_count
):
    count_q = features.shape[0]
    blocks_here = block_len.shape[0]
    block_rows = count_q // blocks_here
    live_flag = (
        (jnp.arange(block_rows, dtype=jnp.int32)[None, :] < block_len[:, None])
        .reshape(count_q)
        .astype(jnp.bfloat16)
    )
    normed = rms_normed(features)
    query = project(normed, w_query)
    intra = intra_branch(query, normed, live_flag, w_key, w_value)
    cross = cross_branch(query, normed, live_flag, w_key, w_value, cross_blocks, cross_count)
    mixed = (intra + cross).astype(jnp.bfloat16)
    resid = (
        features.astype(jnp.float32) + jnp.dot(mixed, w_out, preferred_element_type=jnp.float32)
    ).astype(jnp.bfloat16)
    normed_two = rms_normed(resid)
    hidden = jax.nn.gelu(jnp.dot(normed_two, w_up, preferred_element_type=jnp.float32)).astype(
        jnp.bfloat16
    )
    return (
        resid.astype(jnp.float32) + jnp.dot(hidden, w_down, preferred_element_type=jnp.float32)
    ).astype(jnp.bfloat16)


def solution(mesh):
    return jax.shard_map(
        body,
        mesh=mesh,
        in_specs=(
            P(("group", "dom"), None),
            P(),
            P(),
            P(),
            P(),
            P(),
            P(),
            P(("group", "dom")),
            P(("group", "dom"), None),
            P(("group", "dom")),
        ),
        out_specs=P(("group", "dom"), None),
        check_vma=False,
    )
```

profile of v0, /device:TPU:0, one launch (start us, length us, event | category | flops | bytes accessed | tf_op | source)
XLA Modules:
  0.0 300.1 jit_solution(13028770647388802317)
XLA Ops:
  6.5 0.0 copy-start
  6.5 0.0 all-gather.6.cloned.1.call-start
  6.6 1.4 copy.47
  8.0 0.0 copy-start.1
  8.0 0.2 fusion.47
  8.2 0.9 fusion.48
  9.1 0.0 all-gather.6.cloned.1.call-update
  9.1 0.0 all-gather.4.cloned.1.call-start
  9.1 0.7 fusion.74
  9.9 1.9 pad_maximum_fusion
  11.8 0.0 all-gather.4.cloned.1.call-update
  11.8 0.0 copy-done.5
  11.8 0.1 copy.48
  11.9 0.0 copy-done.1
  11.9 0.1 reshape.154
  12.0 0.0 copy-done.4
  12.0 1.5 convolution_convert_fusion.4
  13.6 0.1 reshape.146
  13.7 12.0 %all-gather = bf16[8,1,512]{2,1,0:T(2,128)(2,1)S(1)} all-gather(bf16[1,1,512]{2,1,0:T(2,128)(2,1)S(1)} %reshape.187), channel_id=1, replica_groups=mesh['group'=8,'dom'=16] {'group'}, dimensions={0}, use_global_device_ids=true | all-gather | bytes 9216 | tf_op jit(solution)/shard_map/all_gather | solution.py:64
  25.8 0.6 gather_fusion.1
  26.4 0.0 copy-done.9
  26.4 0.1 iota_compare_fusion
  26.5 0.1 and_bitcast_fusion
  26.6 17.2 %all-gather.6.cloned.1.call-done = bf16[4096,512]{0,1:T(8,128)(2,1)} async-done(((bf16[512,512]{0,1:T(8,128)(2,1)}), bf16[4096,512]{0,1:T(8,128)(2,1)}) %all-gather.6.cloned.1.call-update) | async-done | bytes 4194320 | tf_op jit(solution)/shard_map/all_gather | solution.py:63
  43.8 6.7 %convolution_convert_fusion.2 = bf16[4096,512]{1,0:T(8,128)(2,1)} fusion(bf16[4096,512]{0,1:T(8,128)(2,1)} %all-gather.6.cloned.1.call-done, bf16[512,512]{1,0:T(8,128)(2,1)} %param.12), kind=kOutput, calls=%fused_computation.16 | convolution fusion | flops 2149580800 | bytes 8912896 | tf_op jit(solution)/shard_map/dot_general | solution.py:30
  50.4 3.8 %gather_fusion.2 = bf16[8,128,512]{2,1,0:T(8,128)(2,1)} fusion(bf16[32,128,512]{2,1,0:T(8,128)(2,1)} %bitcast.59, s32[1024]{0:T(1024)S(1)} %pad_clamp_fusion), kind=kCustom, calls=%fused_computation.2 | custom fusion | bytes 2097184 | tf_op jit(solution)/shard_map/gather | solution.py:72
  54.2 3.9 %reshape.192 = bf16[4,256,8,64]{3,2,1,0:T(8,128)(2,1)} reshape(bf16[8,128,512]{2,1,0:T(8,128)(2,1)} %gather_fusion.2) | data formatting | bytes 2097152 | tf_op jit(solution)/shard_map/reshape | solution.py:72
  58.1 6.7 %convolution_convert_fusion.3 = bf16[4096,512]{1,0:T(8,128)(2,1)} fusion(bf16[4096,512]{0,1:T(8,128)(2,1)} %all-gather.6.cloned.1.call-done, bf16[512,512]{1,0:T(8,128)(2,1)} %param.13), kind=kOutput, calls=%fused_computation.17 | convolution fusion | flops 2149580800 | bytes 8912896 | tf_op jit(solution)/shard_map/dot_general | solution.py:30
  64.8 3.8 %gather_fusion = bf16[8,128,512]{2,1,0:T(8,128)(2,1)} fusion(bf16[32,128,512]{2,1,0:T(8,128)(2,1)} %bitcast.58, s32[1024]{0:T(1024)S(1)} %pad_clamp_fusion), kind=kCustom, calls=%fused_computation | custom fusion | bytes 2097184 | tf_op jit(solution)/shard_map/gather | solution.py:75
  68.6 3.9 %reshape.191 = bf16[4,256,8,64]{3,2,1,0:T(8,128)(2,1)} reshape(bf16[8,128,512]{2,1,0:T(8,128)(2,1)} %gather_fusion) | data formatting | bytes 2097152 | tf_op jit(solution)/shard_map/reshape | solution.py:75
  72.5 2.3 fusion.18
  74.9 2.1 fusion.75
  77.0 0.0 copy-start.6
  77.0 0.8 fusion.42
  77.8 1.6 copy.54
  79.5 45.6 %all-gather.4.cloned.1.call-done = bf16[8192,513]{0,1:T(8,128)(2,1)} async-done(((bf16[512,513]{0,1:T(8,128)(2,1)}), bf16[8192,513]{0,1:T(8,128)(2,1)}) %all-gather.4.cloned.1.call-update) | async-done | bytes 8405008 | tf_op jit(solution)/shard_map/all_gather | solution.py:17
  125.1 1.0 compare_reduce_fusion
  126.1 0.0 copy-done.6
  126.1 10.2 %convolution_convert_fusion = bf16[8192,512]{0,1:T(8,128)(2,1)} fusion(bf16[512,512]{1,0:T(8,128)(2,1)S(1)} %copy-done.6, bf16[8192,513]{0,1:T(8,128)(2,1)} %all-gather.4.cloned.1.call-done), kind=kOutput, calls=%fused_computation.11 | convolution fusion | flops 4299161600 | bytes 17301504 | tf_op jit(solution)/shard_map/dot_general | solution.py:30
  136.3 47.2 %fusion.1 = (f32[8,512]{1,0:T(8,128)S(1)}, f32[8,512,8192]{2,1,0:T(8,128)}) fusion(pred[8192]{0:T(1024)(128)(4,1)S(1)} %compare_reduce_fusion, bf16[512,8,64]{0,2,1:T(8,128)(2,1)S(1)} %bitcast.56, bf16[8192,8,64]{0,2,1:T(8,128)(2,1)} %bitcast.55), kind=kOutput, calls=%fused_computation.6 | convolution fusion | flops 4395626496 | bytes 143155200 | tf_op jit(solution)/shard_map/rhd,shd->hrs/dot_general | solution.py:46
  183.4 43.6 %fusion.2 = f32[8,512]{1,0:T(8,128)S(1)} fusion(f32[8,512,8192]{2,1,0:T(8,128)} %get-tuple-element.10, f32[8,512]{1,0:T(8,128)S(1)} %broadcast_maximum_fusion, pred[8192]{0:T(1024)(128)(4,1)S(1)} %compare_reduce_fusion), kind=kLoop, calls=%fused_computation.7 | loop fusion | flops 167768064 | bytes 134258688 | tf_op jit(solution)/shard_map/reduce_sum | solution.py:51
  227.1 0.0 copy-done.7
  227.1 10.2 %convolution_convert_fusion.1 = bf16[8192,512]{0,1:T(8,128)(2,1)} fusion(bf16[512,512]{1,0:T(8,128)(2,1)S(1)} %copy-done.7, bf16[8192,513]{0,1:T(8,128)(2,1)} %all-gather.4.cloned.1.call-done), kind=kOutput, calls=%fused_computation.12 | convolution fusion | flops 4299161600 | bytes 17301504 | tf_op jit(solution)/shard_map/dot_general | solution.py:30
  237.3 47.1 %broadcast_divide_fusion = f32[512,8,64]{0,2,1:T(8,128)} fusion(f32[512,8]{0,1:T(8,128)S(1)} %bitcast.60, bf16[8192,8,64]{0,2,1:T(8,128)(2,1)} %bitcast.63, f32[8,512,8192]{2,1,0:T(8,128)} %get-tuple-element.10, f32[8,512]{1,0:T(8,128)S(1)} %broadcast_maximum_fusion, pred[8192]{0:T(1024)(128)(4,1)S(1)} %compare_reduce_fusion), kind=kOutput, calls=%fused_computation.60 | convolution fusion | flops 4463001600 | bytes 143695872 | tf_op jit(solution)/shard_map/hrs,shd->rhd/dot_general | solution.py:52
  284.4 1.7 fusion.51
  286.1 1.3 fusion.49
  287.4 4.8 %fusion.39 = bf16[512,512]{0,1:T(8,128)(2,1)S(1)} fusion(bf16[2048,512]{1,0:T(8,128)(2,1)S(1)} %copy-done, bf16[512,512]{0,1:T(8,128)(2,1)} %get-tuple-element.12, bf16[512,2048]{1,0:T(8,128)(2,1)} %param.15, f32[512]{0:T(512)S(1)} %add_rsqrt_fusion), kind=kOutput, calls=%fused_computation.48 | convolution fusion | flops 2158493696 | bytes 5244928 | tf_op jit(solution)/shard_map/dot_general | solution.py:120
  292.3 1.0 copy.56
  (23 shorter events, 0.2 us)
Async XLA Ops:
  6.5 280.9 %copy-start = (bf16[2048,512]{1,0:T(8,128)(2,1)S(1)}, bf16[2048,512]{1,0:T(8,128)(2,1)}, u32[]{:S(2)}) copy-start(bf16[2048,512]{1,0:T(8,128)(2,1)} %param.16) | copy-start | bytes 6291460
  6.5 5.3 %copy-start.5 = (s32[4,2]{0,1:T(2,128)S(1)}, s32[4,2]{0,1:T(2,128)}, u32[]{:S(2)}) copy-start(s32[4,2]{0,1:T(2,128)} %param.18) | copy-start | bytes 100
  6.5 5.5 %copy-start.4 = (bf16[512,512]{1,0:T(8,128)(2,1)S(1)}, bf16[512,512]{1,0:T(8,128)(2,1)}, u32[]{:S(2)}) copy-start(bf16[512,512]{1,0:T(8,128)(2,1)} %param.11) | copy-start | bytes 1572868
  6.5 19.9 %copy-start.9 = (s32[4]{0:T(128)S(1)}, s32[4]{0:T(128)}, u32[]{:S(2)}) copy-start(s32[4]{0:T(128)} %param.19) | copy-start | bytes 52
  6.5 37.2 %all-gather.6.cloned.1.call-start = ((), (), s32[]{:S(2)}) async-start(), calls=%async_computation.1 | async-start | bytes 4718592 | tf_op jit(solution)/shard_map/all_gather | solution.py:63
  8.0 4.0 %copy-start.1 = (bf16[512,512]{0,1:T(8,128)(2,1)}, bf16[512,512]{0,1:T(8,128)(2,1)S(1)}, u32[]{:S(2)}) copy-start(bf16[512,512]{0,1:T(8,128)(2,1)S(1)} %copy.47) | copy-start | bytes 1572868
  9.1 116.0 %all-gather.4.cloned.1.call-start = ((), (), s32[]{:S(2)}) async-start(), calls=%async_computation | async-start | bytes 9052160 | tf_op jit(solution)/shard_map/all_gather | solution.py:17
  74.9 2.1 copy-start.3
  77.0 49.1 %copy-start.6 = (bf16[512,512]{1,0:T(8,128)(2,1)S(1)}, bf16[512,512]{1,0:T(8,128)(2,1)}, u32[]{:S(2)}) copy-start(bf16[512,512]{1,0:T(8,128)(2,1)} %param.12) | copy-start | bytes 1572868
  183.4 43.6 %copy-start.7 = (bf16[512,512]{1,0:T(8,128)(2,1)S(1)}, bf16[512,512]{1,0:T(8,128)(2,1)}, u32[]{:S(2)}) copy-start(bf16[512,512]{1,0:T(8,128)(2,1)} %param.13) | copy-start | bytes 1572868
  237.3 48.8 %copy-start.2 = (bf16[512,512]{0,1:T(8,128)(2,1)S(1)}, bf16[512,512]{0,1:T(8,128)(2,1)}, u32[]{:S(2)}) copy-start(bf16[512,512]{0,1:T(8,128)(2,1)} %copy-done.1) | copy-start | bytes 1572868
  237.3 48.8 %copy-start.8 = (bf16[512,512]{1,0:T(8,128)(2,1)S(1)}, bf16[512,512]{1,0:T(8,128)(2,1)}, u32[]{:S(2)}) copy-start(bf16[512,512]{1,0:T(8,128)(2,1)} %param.14) | copy-start | bytes 1572868
Sparse Core Ops, SparseCore 0:
  9.2 34.5 all-gather.5
  45.9 79.1 all-gather.3
where the time goes:
time: 301 us; the launch traced here: 300 us
  matrix products  139 us (46%)
  waiting for transfers between devices  62.8 us (21%)
  other arithmetic  52.4 us (17%)
  local copies, waits for them, and re-layouts  20.5 us (7%)
  between operations  13.6 us (5%)
  blocking collectives  12 us (4%)
    dot_general x1, matrix products, intra_branch(): jnp.einsum('rhd,shd->hrs', q_heads, k_heads, preferred_element_type=jnp.f...  47.2 us
    dot_general x1, matrix products, intra_branch(): jnp.einsum('hrs,shd->rhd', weights.astype(jnp.bfloat16), v_heads, preferr...  47.1 us
    all_gather x1, waiting for transfers between devices, in_one_piece(): whole = lax.all_gather(both, axis, axis=dim, tiled=True)  45.6 us
    reduce_sum x1, other arithmetic, intra_branch(): total_new = jnp.sum(weights, axis=-1)  43.6 us
    dot_general x5, matrix products, project(): jnp.dot(rows, weight, preferred_element_type=jnp.float32)  35.2 us
    all_gather x1, waiting for transfers between devices, cross_branch(): lax.all_gather(normed, 'group', axis=0, tiled=True)  17.2 us
    all_gather x1, blocking collectives, cross_branch(): lax.all_gather(live_flag, 'group', axis=0, tiled=True)  12 us
  transfers between devices with their start and end apart: 2, of which 2 were waited for; matrix products, arithmetic and copies ran while one was open for 14% of the time, Pallas kernels for 0%

commit v1 on v0

v1 whole, which is shorter than its diff:
```python
import functools
import math

import jax
import jax.numpy as jnp
from jax import lax
from jax.experimental import pallas as pl
from jax.experimental.pallas import tpu as pltpu
from jax.sharding import PartitionSpec as P

F32, BF16 = jnp.float32, jnp.bfloat16
MESH = pl.DeviceIdType.MESH
HEADS = 8
HEAD = 64
BLK = 128
TOK = 512
D = 512
FF = 2048
VROWS = 80
ROUNDS = 16
NEG = -1e30
FLAG = 64.0
SOURCE = (
    (0, 0), (0, 1), (1, 0), (1, 1), (3, 0), (2, 0), (3, 1), (4, 0),
    (5, 1), (6, 0), (7, 0), (8, 0), (9, 0), (11, 0), (13, 0),
)


def dot(a, b):
    return jnp.dot(a, b, preferred_element_type=F32)


def dot_t(a, b):
    return lax.dot_general(a, b, (((1,), (1,)), ((), ())), preferred_element_type=F32)


def rms(wide):
    return (wide * lax.rsqrt(jnp.mean(wide * wide, axis=-1, keepdims=True) + 1e-06)).astype(BF16)


def kernel(
    len_ref, blocks_ref, count_ref, x_ref, wq_hbm, wk_hbm, wv_hbm, wo_hbm, wup_hbm, wdown_hbm,
    out_ref,
    wq, wk, wv, wo, wup, wdown, wvt, nrm, own, rbuf, xbuf, qt, ks, vt, acc, top, st, mix, w_sem,
    s_sem, r_sem, xs_sem, xr_sem, bs_sem, br_sem,
):
    weights = [(wq_hbm, wq), (wk_hbm, wk), (wv_hbm, wv), (wo_hbm, wo), (wup_hbm, wup), (wdown_hbm, wdown)]

    def fetch(k):
        return pltpu.make_async_copy(weights[k][0], weights[k][1], w_sem.at[k])

    for k in range(6):
        fetch(k).start()

    g, d = lax.axis_index("group"), lax.axis_index("dom")
    y, z = d // 4, d % 4
    up_y, dn_y = (y + 1) % 4 * 4 + z, (y + 3) % 4 * 4 + z
    up_z, dn_z = y * 4 + (z + 1) % 4, y * 4 + (z + 3) % 4
    towards = [(g, up_y), (g, up_z), (g, dn_y), (g, dn_z)]
    up_x, dn_x, sibling = ((g + 2) % 8, d), ((g + 6) % 8, d), (g + 1 - 2 * (g % 2), d)

    barrier = pltpu.get_barrier_semaphore()
    for other in [*towards, up_x, dn_x, sibling]:
        pl.semaphore_signal(barrier, inc=1, device_id=other, device_id_type=MESH)

    normed = rms(x_ref[...].astype(F32))
    nrm[...] = normed
    row = lax.broadcasted_iota(jnp.int32, (BLK, D), 0)
    lane = lax.broadcasted_iota(jnp.int32, (BLK, D), 1)
    flag = jnp.where((lane == 0) | (lane == 64), FLAG, 0.0)
    for b in range(4):
        part = normed[b * BLK:(b + 1) * BLK].astype(F32)
        flagged = jnp.where(row < len_ref[b], part, flag).astype(BF16)
        rbuf[0, b * BLK:(b + 1) * BLK, :] = flagged
        own[b] = flagged

    pl.semaphore_wait(barrier, 7)

    def send(n, link):
        slot, partner = SOURCE[n]
        return pltpu.make_async_remote_copy(
            src_ref=rbuf.at[slot, pl.ds((link ^ partner) * BLK, BLK)],
            dst_ref=rbuf.at[n + 1, pl.ds(link * BLK, BLK)],
            send_sem=s_sem.at[n, link], recv_sem=r_sem.at[n, link],
            device_id=towards[link], device_id_type=MESH,
        )

    def send_x(s, way):
        blocks = pl.ds(4 * s + 2 * way, 2)
        return pltpu.make_async_remote_copy(
            src_ref=own.at[pl.ds(2 * way, 2)] if s == 0 else xbuf.at[blocks],
            dst_ref=xbuf.at[pl.ds(4 * s + 4 + 2 * way, 2)],
            send_sem=xs_sem.at[s, way], recv_sem=xr_sem.at[s, way],
            device_id=(up_x, dn_x)[way], device_id_type=MESH,
        )

    def send_sibling(s):
        return pltpu.make_async_remote_copy(
            src_ref=own if s == 0 else xbuf.at[pl.ds(4 * s, 4)],
            dst_ref=xbuf.at[pl.ds(16 + 4 * s, 4)],
            send_sem=bs_sem.at[s], recv_sem=br_sem.at[s],
            device_id=sibling, device_id_type=MESH,
        )

    for n in range(2):
        for link in range(4):
            send(n, link).start()
    for way in range(2):
        send_x(0, way).start()
    send_sibling(0).start()

    fetch(0).wait()
    q_all = dot_t(jnp.transpose(wq[...].astype(F32)).astype(BF16), nrm[...]) * (math.log2(math.e) / 8.0)
    q_all = q_all.astype(BF16)
    ones = jnp.ones((HEAD, TOK), BF16)
    for h in range(HEADS):
        at = (h % 2) * HEAD
        qt[h, at:at + HEAD, :] = q_all[h * HEAD:(h + 1) * HEAD]
        qt[h, HEAD - at:HEAD - at + HEAD, :] = ones
        vt[h, HEAD:VROWS, :] = jnp.ones((VROWS - HEAD, TOK), BF16)
    fetch(1).wait()
    fetch(2).wait()
    wvt[...] = jnp.transpose(wv[...].astype(F32)).astype(BF16)
    acc[...] = jnp.zeros_like(acc)
    top[...] = jnp.full_like(top, NEG)

    def keys_of(rows, unused=None):
        n = rows.shape[0]
        ks[0:n, :] = dot(rows, wk[...]).astype(BF16)
        values = dot_t(wvt[...], rows).astype(BF16)
        for h in range(HEADS):
            vt[h, 0:HEAD, 0:n] = values[h * HEAD:(h + 1) * HEAD]
        mask = jnp.where(rows[:, 0:BLK].astype(F32) > FLAG / 2, NEG, 0.0)
        if unused is not None:
            mask = jnp.where(unused, NEG, mask)
        return mask.astype(BF16)

    def scores(h, n, mask, q):
        lane = lax.broadcasted_iota(jnp.int32, (n, BLK), 1)
        pair = ks[0:n, (h // 2) * BLK:(h // 2 + 1) * BLK]
        mine = (lane < HEAD) if h % 2 == 0 else (lane >= HEAD)
        return dot(jnp.where(mine, pair, mask), q)

    def attend(rows):
        mask = keys_of(rows)
        st[0] = scores(0, TOK, mask, qt[0])
        for h in range(HEADS):
            if h + 1 < HEADS:
                st[(h + 1) % 2] = scores(h + 1, TOK, mask, qt[h + 1])
            s = st[h % 2]
            old = top[h]
            new = jnp.maximum(old, jnp.max(s, axis=0, keepdims=True))
            top[h] = new
            p = jnp.exp2(s - new).astype(BF16)
            acc[h] = acc[h] * jnp.exp2(old - new) + dot(vt[h], p)

    def cross(b):
        picked = []
        for c in range(2):
            block = blocks_ref[b, c]
            group, local = lax.div(block, 64), lax.rem(block, 4)
            apart = (lax.div(g, 2) - lax.div(group, 2)) * (1 - 2 * lax.div(local, 2))
            slot = lax.rem(group + g, 2) * 16 + lax.rem(apart + 4, 4) * 4 + local
            picked.append(xbuf[slot])
        rows = jnp.concatenate(picked, axis=0)
        at = lax.broadcasted_iota(jnp.int32, (2 * BLK, BLK), 0) // BLK
        mask = keys_of(rows, at >= count_ref[b])
        here = pl.ds(b * BLK, BLK)
        for h in range(HEADS):
            s = scores(h, 2 * BLK, mask, qt[h, :, here])
            p = jnp.exp2(s - jnp.max(s, axis=0, keepdims=True)).astype(BF16)
            o = dot(vt[h, :, 0:2 * BLK], p)
            mix[h * HEAD:(h + 1) * HEAD, here] = o[0:HEAD] / o[HEAD:HEAD + 1]

    def round_(r, carry):
        for n in range(ROUNDS - 1):
            @pl.when(r == n + 1)
            def _(n=n):
                for link in range(4):
                    send(n, link).wait_recv()
                if n + 2 < ROUNDS - 1:
                    for link in range(4):
                        send(n + 2, link).start()
        for s in range(1, 4):
            @pl.when(r == 1 + 2 * s)
            def _(s=s):
                for way in range(2):
                    send_x(s - 1, way).wait_recv()
                    if s < 3:
                        send_x(s, way).start()
                send_sibling(s).start()
        attend(rbuf[r])
        return carry

    lax.fori_loop(0, ROUNDS, round_, 0)

    for s in range(4):
        send_sibling(s).wait_recv()
    for b in range(4):
        cross(b)

    for n in range(ROUNDS - 1):
        for link in range(4):
            send(n, link).wait_send()
    for s in range(3):
        for way in range(2):
            send_x(s, way).wait_send()
    for s in range(4):
        send_sibling(s).wait_send()

    for h in range(HEADS):
        at = slice(h * HEAD, (h + 1) * HEAD)
        mix[at, :] = mix[at, :] + acc[h, 0:HEAD] / acc[h, HEAD:HEAD + 1]
    mixed = jnp.transpose(mix[...]).astype(BF16)
    for k in range(3, 6):
        fetch(k).wait()
    resid = (x_ref[...].astype(F32) + dot(mixed, wo[...])).astype(BF16)
    normed_two = rms(resid.astype(F32))
    total = resid.astype(F32)
    for k in range(FF // TOK):
        cols = slice(k * TOK, (k + 1) * TOK)
        hidden = jax.nn.gelu(dot(normed_two, wup[:, cols])).astype(BF16)
        total = total + dot(hidden, wdown[cols, :])
    out_ref[...] = total.astype(BF16)


def body(features, w_query, w_key, w_value, w_out, w_up, w_down, block_len, cross_blocks, cross_count):
    smem = pl.BlockSpec(memory_space=pltpu.SMEM)
    vmem = pl.BlockSpec(memory_space=pltpu.VMEM)
    hbm = pl.BlockSpec(memory_space=pl.ANY)
    dma = pltpu.SemaphoreType.DMA
    return pl.pallas_call(
        kernel,
        out_shape=jax.ShapeDtypeStruct((TOK, D), BF16),
        in_specs=[smem] * 3 + [vmem] + [hbm] * 6,
        out_specs=vmem,
        scratch_shapes=[
            pltpu.VMEM((D, D), BF16), pltpu.VMEM((D, D), BF16), pltpu.VMEM((D, D), BF16), pltpu.VMEM((D, D), BF16),
            pltpu.VMEM((D, FF), BF16), pltpu.VMEM((FF, D), BF16),
            pltpu.VMEM((D, D), BF16),
            pltpu.VMEM((TOK, D), BF16),
            pltpu.VMEM((4, BLK, D), BF16),
            pltpu.VMEM((ROUNDS, TOK, D), BF16),
            pltpu.VMEM((32, BLK, D), BF16),
            pltpu.VMEM((HEADS, 2 * HEAD, TOK), BF16),
            pltpu.VMEM((TOK, D), BF16),
            pltpu.VMEM((HEADS, VROWS, TOK), BF16),
            pltpu.VMEM((HEADS, VROWS, TOK), F32),
            pltpu.VMEM((HEADS, 1, TOK), F32),
            pltpu.VMEM((2, TOK, TOK), F32),
            pltpu.VMEM((D, TOK), F32),
            dma((6,)),
            dma((ROUNDS - 1, 4)), dma((ROUNDS - 1, 4)),
            dma((3, 2)), dma((3, 2)), dma((4,)), dma((4,)),
        ],
        compiler_params=pltpu.CompilerParams(
            collective_id=0, has_side_effects=True, vmem_limit_bytes=60 * 2**20
        ),
        name="layer",
    )(block_len, cross_blocks, cross_count, features, w_query, w_key, w_value, w_out, w_up, w_down)


def solution(mesh):
    both = P(("group", "dom"))
    rows = P(("group", "dom"), None)
    return jax.shard_map(
        body,
        mesh=mesh,
        in_specs=(rows, P(), P(), P(), P(), P(), P(), both, rows, both),
        out_specs=rows,
        check_vma=False,
    )
```

time: 301 us -> 84.2 us (0.28)
  matrix products: 139 us -> 0 us
  Pallas kernels: 0 us -> 80.8 us
  waiting for transfers between devices: 62.8 us -> 0 us
  other arithmetic: 52.4 us -> 0 us
  local copies, waits for them, and re-layouts: 20.5 us -> 3.2 us
  between operations: 13.6 us -> 0.01 us
  blocking collectives: 12 us -> 0 us
    dot_general x11 -> x0, matrix products: 139 us -> none  [the longest x1 47.2 us: intra_branch(): jnp.einsum('rhd,shd->hrs', q_heads, k_heads, preferred_element_type=jnp.f...]
    pallas_call x0 -> x1, Pallas kernels: none -> 80.8 us  [body(): pl.pallas_call(kernel, out_shape=jax.ShapeDtypeStruct((TOK, D), BF16), in...]
    all_gather x2 -> x0, waiting for transfers between devices: 62.8 us -> none  [the longest x1 45.6 us: in_one_piece(): whole = lax.all_gather(both, axis, axis=dim, tiled=True)]
    reduce_sum x2 -> x0, other arithmetic: 43.8 us -> none  [the longest x1 43.6 us: intra_branch(): total_new = jnp.sum(weights, axis=-1)]
    all_gather x1 -> x0, blocking collectives: 12 us -> none  [cross_branch(): lax.all_gather(live_flag, 'group', axis=0, tiled=True)]
    gather x3 -> x0, local copies, waits for them, and re-layouts: 8.14 us -> none  [the longest x1 3.8 us: cross_branch(): value_all.reshape(-1, block_rows, width)[chosen]]
    reshape x4 -> x0, local copies, waits for them, and re-layouts: 8 us -> none  [the longest x1 3.94 us: cross_branch(): value_all.reshape(-1, block_rows, width)[chosen]]
  transfers between devices with their start and end apart: 2 -> 0, of which waited for: 2 -> 0; matrix products, arithmetic and copies ran while one was open for 14% -> 0% of each run, Pallas kernels for 0% -> 0%
where the time goes in v1:
time: 84.2 us; the launch traced here: 84 us
  Pallas kernels  80.8 us (96%)
  local copies, waits for them, and re-layouts  3.2 us (4%)
    pallas_call x1, Pallas kernels, body(): pl.pallas_call(kernel, out_shape=jax.ShapeDtypeStruct((TOK, D), BF16), in...  80.8 us
    unnamed x2, local copies, waits for them, and re-layouts  3.2 us

profile of v1, /device:TPU:0, one launch (start us, length us, event | category | flops | bytes accessed | tf_op | source)
XLA Modules:
  0.0 84.0 jit_solution(3973793620323876915)
XLA Ops:
  0.0 1.3 %copy.11.blocks_ref = s32[4,2]{1,0:T(4,128)} copy(s32[4,2]{0,1:T(2,128)} %param.18) | data formatting | bytes 64 | tf_op args[8]
  1.3 80.8 %layer.1 = bf16[512,512]{1,0:T(8,128)(2,1)} custom-call(s32[4]{0:T(128)} %len_ref.1, s32[4,2]{1,0:T(4,128)} %copy.11.blocks_ref, s32[4]{0:T(128)} %count_ref.1, bf16[512,512]{1,0:T(8,128)(2,1)} %x_ref.1, bf16[512,512]{1,0:T(8,128)(2,1)} %wq_hbm.1, bf16[512,512]{1,0:T(8,128)(2,1)} %wk_hbm.1, bf16[512,512]{1,0:T(8,128)(2,1)} %wv_hbm.1, ...), custom_call_target="tpu_custom_call" | custom-call | tf_op jit(solution)/shard_map/layer/pallas_call | solution.py:232
  82.2 1.9 %copy.13 = bf16[512,512]{1,0:T(8,128)(2,1)} copy(bf16[512,512]{1,0:T(8,128)(2,1)} %layer.1) | data formatting | bytes 1048576

commit v2 on v1

--- a/solution.py
+++ b/solution.py
@@ -21,8 +21,8 @@
 NEG = -1e30
 FLAG = 64.0
 SOURCE = (
-    (0, 0), (0, 1), (1, 0), (1, 1), (3, 0), (2, 0), (3, 1), (4, 0),
-    (5, 1), (6, 0), (7, 0), (8, 0), (9, 0), (11, 0), (13, 0),
+    (-1, 0), (-1, 2), (-1, 1), (-1, 3), (0, 0), (0, 1), (0, 3), (1, 3),
+    (1, 1), (2, 0), (4, 1), (4, 3), (5, 0), (7, 0), (10, 0),
 )
 
 
@@ -41,7 +41,7 @@
 def kernel(
     len_ref, blocks_ref, count_ref, x_ref, wq_hbm, wk_hbm, wv_hbm, wo_hbm, wup_hbm, wdown_hbm,
     out_ref,
-    wq, wk, wv, wo, wup, wdown, wvt, nrm, own, rbuf, xbuf, qt, ks, vt, acc, top, st, mix, w_sem,
+    wq, wk, wv, wo, wup, wdown, wvt, nrm, own, rbuf, xbuf, qt, ks, vt, acc, top, chunk_top, st, ps, mix, w_sem,
     s_sem, r_sem, xs_sem, xr_sem, bs_sem, br_sem,
 ):
     weights = [(wq_hbm, wq), (wk_hbm, wk), (wv_hbm, wv), (wo_hbm, wo), (wup_hbm, wup), (wdown_hbm, wdown)]
@@ -49,7 +49,7 @@
     def fetch(k):
         return pltpu.make_async_copy(weights[k][0], weights[k][1], w_sem.at[k])
 
-    for k in range(6):
+    for k in range(3):
         fetch(k).start()
 
     g, d = lax.axis_index("group"), lax.axis_index("dom")
@@ -71,24 +71,34 @@
     for b in range(4):
         part = normed[b * BLK:(b + 1) * BLK].astype(F32)
         flagged = jnp.where(row < len_ref[b], part, flag).astype(BF16)
-        rbuf[0, b * BLK:(b + 1) * BLK, :] = flagged
+        rbuf[b * BLK:(b + 1) * BLK, :] = flagged
         own[b] = flagged
 
     pl.semaphore_wait(barrier, 7)
 
     def send(n, link):
-        slot, partner = SOURCE[n]
+        arrival, other = SOURCE[n]
         return pltpu.make_async_remote_copy(
-            src_ref=rbuf.at[slot, pl.ds((link ^ partner) * BLK, BLK)],
-            dst_ref=rbuf.at[n + 1, pl.ds(link * BLK, BLK)],
+            src_ref=rbuf.at[pl.ds((arrival + 1) * TOK + (link ^ other) * BLK, BLK)],
+            dst_ref=rbuf.at[pl.ds((n + 1) * TOK + link * BLK, BLK)],
             send_sem=s_sem.at[n, link], recv_sem=r_sem.at[n, link],
             device_id=towards[link], device_id_type=MESH,
         )
 
+    def start_after(arrival):
+        for n in range(ROUNDS - 1):
+            if SOURCE[n][0] == arrival:
+                for link in range(4):
+                    send(n, link).start()
+
+    def step(arrival):
+        for link in range(4):
+            send(arrival, link).wait_recv()
+        start_after(arrival)
+
     def send_x(s, way):
-        blocks = pl.ds(4 * s + 2 * way, 2)
         return pltpu.make_async_remote_copy(
-            src_ref=own.at[pl.ds(2 * way, 2)] if s == 0 else xbuf.at[blocks],
+            src_ref=own.at[pl.ds(2 * way, 2)] if s == 0 else xbuf.at[pl.ds(4 * s + 2 * way, 2)],
             dst_ref=xbuf.at[pl.ds(4 * s + 4 + 2 * way, 2)],
             send_sem=xs_sem.at[s, way], recv_sem=xr_sem.at[s, way],
             device_id=(up_x, dn_x)[way], device_id_type=MESH,
@@ -102,12 +112,19 @@
             device_id=sibling, device_id_type=MESH,
         )
 
-    for n in range(2):
-        for link in range(4):
-            send(n, link).start()
+    def step_x(s):
+        for way in range(2):
+            send_x(s - 1, way).wait_recv()
+            if s < 3:
+                send_x(s, way).start()
+        send_sibling(s).start()
+
+    start_after(-1)
     for way in range(2):
         send_x(0, way).start()
     send_sibling(0).start()
+    for k in range(3, 6):
+        fetch(k).start()
 
     fetch(0).wait()
     q_all = dot_t(jnp.transpose(wq[...].astype(F32)).astype(BF16), nrm[...]) * (math.log2(math.e) / 8.0)
@@ -117,7 +134,7 @@
         at = (h % 2) * HEAD
         qt[h, at:at + HEAD, :] = q_all[h * HEAD:(h + 1) * HEAD]
         qt[h, HEAD - at:HEAD - at + HEAD, :] = ones
-        vt[h, HEAD:VROWS, :] = jnp.ones((VROWS - HEAD, TOK), BF16)
+        vt[h, HEAD:VROWS, :] = jnp.ones((VROWS - HEAD, 2 * TOK), BF16)
     fetch(1).wait()
     fetch(2).wait()
     wvt[...] = jnp.transpose(wv[...].astype(F32)).astype(BF16)
@@ -135,69 +152,93 @@
             mask = jnp.where(unused, NEG, mask)
         return mask.astype(BF16)
 
-    def scores(h, n, mask, q):
+    def scores(h, at, n, mask, q):
         lane = lax.broadcasted_iota(jnp.int32, (n, BLK), 1)
-        pair = ks[0:n, (h // 2) * BLK:(h // 2 + 1) * BLK]
+        pair = ks[at:at + n, (h // 2) * BLK:(h // 2 + 1) * BLK]
         mine = (lane < HEAD) if h % 2 == 0 else (lane >= HEAD)
-        return dot(jnp.where(mine, pair, mask), q)
+        return dot(jnp.where(mine, pair, mask[at:at + n]), q)
+
+    def pipeline(units, first, second, third):
+        first(0)
+        first(1)
+        second(0)
+        for u in range(units):
+            if u + 1 < units:
+                second(u + 1)
+            if u + 2 < units:
+                first(u + 2)
+            third(u)
 
     def attend(rows):
+        n = rows.shape[0]
         mask = keys_of(rows)
-        st[0] = scores(0, TOK, mask, qt[0])
-        for h in range(HEADS):
-            if h + 1 < HEADS:
-                st[(h + 1) % 2] = scores(h + 1, TOK, mask, qt[h + 1])
-            s = st[h % 2]
+
+        def first(h):
+            s = scores(h, 0, n, mask, qt[h])
+            st[h % 2, 0:n] = s
+            chunk_top[h % 2] = jnp.max(s.reshape(n // 8, 8, TOK), axis=0)
+
+        def second(h):
             old = top[h]
-            new = jnp.maximum(old, jnp.max(s, axis=0, keepdims=True))
+            new = jnp.maximum(old, jnp.max(chunk_top[h % 2], axis=0, keepdims=True))
             top[h] = new
-            p = jnp.exp2(s - new).astype(BF16)
-            acc[h] = acc[h] * jnp.exp2(old - new) + dot(vt[h], p)
-
-    def cross(b):
-        picked = []
-        for c in range(2):
-            block = blocks_ref[b, c]
-            group, local = lax.div(block, 64), lax.rem(block, 4)
-            apart = (lax.div(g, 2) - lax.div(group, 2)) * (1 - 2 * lax.div(local, 2))
-            slot = lax.rem(group + g, 2) * 16 + lax.rem(apart + 4, 4) * 4 + local
-            picked.append(xbuf[slot])
-        rows = jnp.concatenate(picked, axis=0)
-        at = lax.broadcasted_iota(jnp.int32, (2 * BLK, BLK), 0) // BLK
-        mask = keys_of(rows, at >= count_ref[b])
-        here = pl.ds(b * BLK, BLK)
-        for h in range(HEADS):
-            s = scores(h, 2 * BLK, mask, qt[h, :, here])
-            p = jnp.exp2(s - jnp.max(s, axis=0, keepdims=True)).astype(BF16)
-            o = dot(vt[h, :, 0:2 * BLK], p)
-            mix[h * HEAD:(h + 1) * HEAD, here] = o[0:HEAD] / o[HEAD:HEAD + 1]
+            ps[h % 2, 0:n] = jnp.exp2(st[h % 2, 0:n] - new).astype(BF16)
+            acc[h] = acc[h] * jnp.exp2(old - new)
+
+        def third(h):
+            acc[h] += dot(vt[h, :, 0:n], ps[h % 2, 0:n])
+
+        pipeline(HEADS, first, second, third)
+
+    def cross():
+        picked, unused = [], []
+        for b in range(4):
+            for c in range(2):
+                block = blocks_ref[c, b]
+                group, local = lax.div(block, 64), lax.rem(block, 4)
+                apart = (lax.div(g, 2) - lax.div(group, 2)) * (1 - 2 * lax.div(local, 2))
+                slot = lax.rem(group + g, 2) * 16 + lax.rem(apart + 4, 4) * 4 + local
+                picked.append(xbuf[slot])
+            at = lax.broadcasted_iota(jnp.int32, (2 * BLK, BLK), 0) // BLK
+            unused.append(at >= count_ref[b])
+        mask = keys_of(jnp.concatenate(picked, axis=0), jnp.concatenate(unused, axis=0))
+        n = 2 * BLK
+
+        def first(u):
+            h, b = u % HEADS, u // HEADS
+            st[u % 2, 0:n, 0:BLK] = scores(h, b * n, n, mask, qt[h, :, b * BLK:(b + 1) * BLK])
+
+        def second(u):
+            s = st[u % 2, 0:n, 0:BLK]
+            ps[u % 2, 0:n, 0:BLK] = jnp.exp2(s - jnp.max(s, axis=0, keepdims=True)).astype(BF16)
+
+        def third(u):
+            h, b = u % HEADS, u // HEADS
+            o = dot(vt[h, :, b * n:(b + 1) * n], ps[u % 2, 0:n, 0:BLK])
+            mix[h * HEAD:(h + 1) * HEAD, b * BLK:(b + 1) * BLK] = o[0:HEAD] / o[HEAD:HEAD + 1]
+
+        pipeline(4 * HEADS, first, second, third)
+
+    attend(rbuf[0:TOK, :])
 
     def round_(r, carry):
-        for n in range(ROUNDS - 1):
-            @pl.when(r == n + 1)
-            def _(n=n):
-                for link in range(4):
-                    send(n, link).wait_recv()
-                if n + 2 < ROUNDS - 1:
-                    for link in range(4):
-                        send(n + 2, link).start()
-        for s in range(1, 4):
-            @pl.when(r == 1 + 2 * s)
-            def _(s=s):
-                for way in range(2):
-                    send_x(s - 1, way).wait_recv()
-                    if s < 3:
-                        send_x(s, way).start()
-                send_sibling(s).start()
-        attend(rbuf[r])
+        for k in range(1, 8):
+            @pl.when(r == k)
+            def _(k=k):
+                step(2 * k - 2)
+                step(2 * k - 1)
+                if 2 <= k < 5:
+                    step_x(k - 1)
+        attend(rbuf[pl.ds(pl.multiple_of((2 * r - 1) * TOK, TOK), 2 * TOK), :])
         return carry
 
-    lax.fori_loop(0, ROUNDS, round_, 0)
+    lax.fori_loop(1, 8, round_, 0)
 
     for s in range(4):
         send_sibling(s).wait_recv()
-    for b in range(4):
-        cross(b)
+    cross()
+    step(ROUNDS - 2)
+    attend(rbuf[(ROUNDS - 1) * TOK:ROUNDS * TOK, :])
 
     for n in range(ROUNDS - 1):
         for link in range(4):
@@ -240,14 +281,16 @@
             pltpu.VMEM((D, D), BF16),
             pltpu.VMEM((TOK, D), BF16),
             pltpu.VMEM((4, BLK, D), BF16),
-            pltpu.VMEM((ROUNDS, TOK, D), BF16),
+            pltpu.VMEM((ROUNDS * TOK, D), BF16),
             pltpu.VMEM((32, BLK, D), BF16),
             pltpu.VMEM((HEADS, 2 * HEAD, TOK), BF16),
-            pltpu.VMEM((TOK, D), BF16),
-            pltpu.VMEM((HEADS, VROWS, TOK), BF16),
+            pltpu.VMEM((2 * TOK, D), BF16),
+            pltpu.VMEM((HEADS, VROWS, 2 * TOK), BF16),
             pltpu.VMEM((HEADS, VROWS, TOK), F32),
             pltpu.VMEM((HEADS, 1, TOK), F32),
-            pltpu.VMEM((2, TOK, TOK), F32),
+            pltpu.VMEM((2, 8, TOK), F32),
+            pltpu.VMEM((2, 2 * TOK, TOK), F32),
+            pltpu.VMEM((2, 2 * TOK, TOK), BF16),
             pltpu.VMEM((D, TOK), F32),
             dma((6,)),
             dma((ROUNDS - 1, 4)), dma((ROUNDS - 1, 4)),
@@ -257,7 +300,7 @@
             collective_id=0, has_side_effects=True, vmem_limit_bytes=60 * 2**20
         ),
         name="layer",
-    )(block_len, cross_blocks, cross_count, features, w_query, w_key, w_value, w_out, w_up, w_down)
+    )(block_len, cross_blocks.T, cross_count, features, w_query, w_key, w_value, w_out, w_up, w_down)
 
 
 def solution(mesh):

time: 84.2 us -> 73.3 us (0.87)
  Pallas kernels: 80.8 us -> 71.3 us
  local copies, waits for them, and re-layouts: 3.2 us -> 1.87 us
    pallas_call x1, Pallas kernels: 80.8 us -> 71.3 us  [body(): pl.pallas_call(kernel, out_shape=jax.ShapeDtypeStruct((TOK, D), BF16), in...]
    unnamed x2 -> x1, local copies, waits for them, and re-layouts: 3.2 us -> 1.87 us
where the time goes in v2:
time: 73.3 us; the launch traced here: 73.2 us
  Pallas kernels  71.3 us (97%)
  local copies, waits for them, and re-layouts  1.87 us (3%)
    pallas_call x1, Pallas kernels, body(): pl.pallas_call(kernel, out_shape=jax.ShapeDtypeStruct((TOK, D), BF16), in...  71.3 us
    unnamed x1, local copies, waits for them, and re-layouts  1.87 us

profile of v2, /device:TPU:0, one launch (start us, length us, event | category | flops | bytes accessed | tf_op | source)
XLA Modules:
  0.0 73.2 jit_solution(12196404587472190)
XLA Ops:
  0.0 71.3 %layer.1 = bf16[512,512]{1,0:T(8,128)(2,1)} custom-call(s32[4]{0:T(128)} %len_ref.1, s32[2,4]{1,0:T(2,128)} %bitcast.1, s32[4]{0:T(128)} %count_ref.1, bf16[512,512]{1,0:T(8,128)(2,1)} %x_ref.1, bf16[512,512]{1,0:T(8,128)(2,1)} %wq_hbm.1, bf16[512,512]{1,0:T(8,128)(2,1)} %wk_hbm.1, bf16[512,512]{1,0:T(8,128)(2,1)} %wv_hbm.1, bf16[512,512]{1,0:T(8,128)(2,1)} %wo_hbm.1, ...), custom_call_target="tpu_custom_call" | custom-call | tf_op jit(solution)/shard_map/layer/pallas_call | solution.py:273
  71.3 1.9 %copy.12 = bf16[512,512]{1,0:T(8,128)(2,1)} copy(bf16[512,512]{1,0:T(8,128)(2,1)} %layer.1) | data formatting | bytes 1048576

commit v3 on v2

--- a/solution.py
+++ b/solution.py
@@ -85,16 +85,14 @@
             device_id=towards[link], device_id_type=MESH,
         )
 
-    def start_after(arrival):
-        for n in range(ROUNDS - 1):
-            if SOURCE[n][0] == arrival:
-                for link in range(4):
-                    send(n, link).start()
-
-    def step(arrival):
+    def start(n):
+        if n < ROUNDS - 1:
+            for link in range(4):
+                send(n, link).start()
+
+    def arrive(n):
         for link in range(4):
-            send(arrival, link).wait_recv()
-        start_after(arrival)
+            send(n, link).wait_recv()
 
     def send_x(s, way):
         return pltpu.make_async_remote_copy(
@@ -119,7 +117,7 @@
                 send_x(s, way).start()
         send_sibling(s).start()
 
-    start_after(-1)
+    start(0)
     for way in range(2):
         send_x(0, way).start()
     send_sibling(0).start()
@@ -219,25 +217,50 @@
 
         pipeline(4 * HEADS, first, second, third)
 
-    attend(rbuf[0:TOK, :])
-
-    def round_(r, carry):
-        for k in range(1, 8):
+    start(1)
+
+    def single(r, carry):
+        @pl.when(r == 1)
+        def _():
+            start(2)
+            arrive(0)
+            start(3)
+            start(4)
+
+        @pl.when(r == 2)
+        def _():
+            arrive(1)
+            start(5)
+            start(6)
+
+        attend(rbuf[pl.ds(pl.multiple_of(r * TOK, TOK), TOK), :])
+        return carry
+
+    lax.fori_loop(0, 3, single, 0)
+
+    def double(r, carry):
+        for k in range(6):
             @pl.when(r == k)
             def _(k=k):
-                step(2 * k - 2)
-                step(2 * k - 1)
-                if 2 <= k < 5:
-                    step_x(k - 1)
-        attend(rbuf[pl.ds(pl.multiple_of((2 * r - 1) * TOK, TOK), 2 * TOK), :])
+                arrive(2 * k + 2)
+                if k < 3:
+                    start(2 * k + 7)
+                arrive(2 * k + 3)
+                if k < 3:
+                    start(2 * k + 8)
+                else:
+                    start(k + 10)
+                if k in (0, 2, 4):
+                    step_x(k // 2 + 1)
+        attend(rbuf[pl.ds(pl.multiple_of((2 * r + 3) * TOK, TOK), 2 * TOK), :])
         return carry
 
-    lax.fori_loop(1, 8, round_, 0)
+    lax.fori_loop(0, 6, double, 0)
 
     for s in range(4):
         send_sibling(s).wait_recv()
     cross()
-    step(ROUNDS - 2)
+    arrive(ROUNDS - 2)
     attend(rbuf[(ROUNDS - 1) * TOK:ROUNDS * TOK, :])
 
     for n in range(ROUNDS - 1):

time: 73.3 us -> 71.7 us (0.978)
  Pallas kernels: 71.3 us -> 69.7 us
    pallas_call x1, Pallas kernels: 71.3 us -> 69.7 us  [body(): pl.pallas_call(kernel, out_shape=jax.ShapeDtypeStruct((TOK, D), BF16), in...]
where the time goes in v3:
time: 71.7 us; the launch traced here: 71.5 us
  Pallas kernels  69.7 us (97%)
  local copies, waits for them, and re-layouts  1.87 us (3%)
    pallas_call x1, Pallas kernels, body(): pl.pallas_call(kernel, out_shape=jax.ShapeDtypeStruct((TOK, D), BF16), in...  69.7 us
    unnamed x1, local copies, waits for them, and re-layouts  1.87 us

profile of v3, /device:TPU:0, one launch (start us, length us, event | category | flops | bytes accessed | tf_op | source)
XLA Modules:
  0.0 71.5 jit_solution(13603600478969505722)
XLA Ops:
  0.0 69.7 %layer.1 = bf16[512,512]{1,0:T(8,128)(2,1)} custom-call(s32[4]{0:T(128)} %len_ref.1, s32[2,4]{1,0:T(2,128)} %bitcast.1, s32[4]{0:T(128)} %count_ref.1, bf16[512,512]{1,0:T(8,128)(2,1)} %x_ref.1, bf16[512,512]{1,0:T(8,128)(2,1)} %wq_hbm.1, bf16[512,512]{1,0:T(8,128)(2,1)} %wk_hbm.1, bf16[512,512]{1,0:T(8,128)(2,1)} %wv_hbm.1, bf16[512,512]{1,0:T(8,128)(2,1)} %wo_hbm.1, ...), custom_call_target="tpu_custom_call" | custom-call | tf_op jit(solution)/shard_map/layer/pallas_call | solution.py:296
  69.7 1.9 %copy.12 = bf16[512,512]{1,0:T(8,128)(2,1)} copy(bf16[512,512]{1,0:T(8,128)(2,1)} %layer.1) | data formatting | bytes 1048576

commit v4 on v3

--- a/solution.py
+++ b/solution.py
@@ -76,12 +76,23 @@
 
     pl.semaphore_wait(barrier, 7)
 
+    def whole(ref, sem):
+        return pltpu.make_async_remote_copy(
+            src_ref=ref, dst_ref=ref, send_sem=sem, recv_sem=sem, device_id=sibling, device_id_type=MESH
+        )
+
+    def landed(ref, sem):
+        whole(ref, sem).wait_recv()
+
+    def left(ref, sem):
+        whole(ref, sem).wait_send()
+
     def send(n, link):
         arrival, other = SOURCE[n]
         return pltpu.make_async_remote_copy(
             src_ref=rbuf.at[pl.ds((arrival + 1) * TOK + (link ^ other) * BLK, BLK)],
             dst_ref=rbuf.at[pl.ds((n + 1) * TOK + link * BLK, BLK)],
-            send_sem=s_sem.at[n, link], recv_sem=r_sem.at[n, link],
+            send_sem=s_sem, recv_sem=r_sem.at[n],
             device_id=towards[link], device_id_type=MESH,
         )
 
@@ -91,14 +102,13 @@
                 send(n, link).start()
 
     def arrive(n):
-        for link in range(4):
-            send(n, link).wait_recv()
+        landed(rbuf.at[pl.ds((n + 1) * TOK, TOK)], r_sem.at[n])
 
     def send_x(s, way):
         return pltpu.make_async_remote_copy(
             src_ref=own.at[pl.ds(2 * way, 2)] if s == 0 else xbuf.at[pl.ds(4 * s + 2 * way, 2)],
             dst_ref=xbuf.at[pl.ds(4 * s + 4 + 2 * way, 2)],
-            send_sem=xs_sem.at[s, way], recv_sem=xr_sem.at[s, way],
+            send_sem=xs_sem, recv_sem=xr_sem.at[s],
             device_id=(up_x, dn_x)[way], device_id_type=MESH,
         )
 
@@ -106,14 +116,14 @@
         return pltpu.make_async_remote_copy(
             src_ref=own if s == 0 else xbuf.at[pl.ds(4 * s, 4)],
             dst_ref=xbuf.at[pl.ds(16 + 4 * s, 4)],
-            send_sem=bs_sem.at[s], recv_sem=br_sem.at[s],
+            send_sem=bs_sem, recv_sem=br_sem,
             device_id=sibling, device_id_type=MESH,
         )
 
     def step_x(s):
-        for way in range(2):
-            send_x(s - 1, way).wait_recv()
-            if s < 3:
+        landed(xbuf.at[pl.ds(4 * s, 4)], xr_sem.at[s - 1])
+        if s < 3:
+            for way in range(2):
                 send_x(s, way).start()
         send_sibling(s).start()
 
@@ -257,20 +267,14 @@
 
     lax.fori_loop(0, 6, double, 0)
 
-    for s in range(4):
-        send_sibling(s).wait_recv()
+    landed(xbuf.at[pl.ds(16, 16)], br_sem)
     cross()
     arrive(ROUNDS - 2)
     attend(rbuf[(ROUNDS - 1) * TOK:ROUNDS * TOK, :])
 
-    for n in range(ROUNDS - 1):
-        for link in range(4):
-            send(n, link).wait_send()
-    for s in range(3):
-        for way in range(2):
-            send_x(s, way).wait_send()
-    for s in range(4):
-        send_sibling(s).wait_send()
+    left(rbuf.at[pl.ds(0, (ROUNDS - 1) * TOK)], s_sem)
+    left(xbuf.at[pl.ds(0, 12)], xs_sem)
+    left(xbuf.at[pl.ds(0, 16)], bs_sem)
 
     for h in range(HEADS):
         at = slice(h * HEAD, (h + 1) * HEAD)
@@ -316,8 +320,8 @@
             pltpu.VMEM((2, 2 * TOK, TOK), BF16),
             pltpu.VMEM((D, TOK), F32),
             dma((6,)),
-            dma((ROUNDS - 1, 4)), dma((ROUNDS - 1, 4)),
-            dma((3, 2)), dma((3, 2)), dma((4,)), dma((4,)),
+            dma, dma((ROUNDS - 1,)),
+            dma, dma((3,)), dma, dma,
         ],
         compiler_params=pltpu.CompilerParams(
             collective_id=0, has_side_effects=True, vmem_limit_bytes=60 * 2**20

time: 71.7 us -> 70.4 us (0.982)
  Pallas kernels: 69.7 us -> 68.3 us
    pallas_call x1, Pallas kernels: 69.7 us -> 68.3 us  [body(): pl.pallas_call(kernel, out_shape=jax.ShapeDtypeStruct((TOK, D), BF16), in...]
where the time goes in v4:
time: 70.4 us; the launch traced here: 70.2 us
  Pallas kernels  68.3 us (97%)
  local copies, waits for them, and re-layouts  1.87 us (3%)
    pallas_call x1, Pallas kernels, body(): pl.pallas_call(kernel, out_shape=jax.ShapeDtypeStruct((TOK, D), BF16), in...  68.3 us
    unnamed x1, local copies, waits for them, and re-layouts  1.87 us

profile of v4, /device:TPU:0, one launch (start us, length us, event | category | flops | bytes accessed | tf_op | source)
XLA Modules:
  0.0 70.2 jit_solution(15779371104538940839)
XLA Ops:
  0.0 68.3 %layer.1 = bf16[512,512]{1,0:T(8,128)(2,1)} custom-call(s32[4]{0:T(128)} %len_ref.1, s32[2,4]{1,0:T(2,128)} %bitcast.1, s32[4]{0:T(128)} %count_ref.1, bf16[512,512]{1,0:T(8,128)(2,1)} %x_ref.1, bf16[512,512]{1,0:T(8,128)(2,1)} %wq_hbm.1, bf16[512,512]{1,0:T(8,128)(2,1)} %wk_hbm.1, bf16[512,512]{1,0:T(8,128)(2,1)} %wv_hbm.1, bf16[512,512]{1,0:T(8,128)(2,1)} %wo_hbm.1, ...), custom_call_target="tpu_custom_call" | custom-call | tf_op jit(solution)/shard_map/layer/pallas_call | solution.py:300
  68.3 1.9 %copy.12 = bf16[512,512]{1,0:T(8,128)(2,1)} copy(bf16[512,512]{1,0:T(8,128)(2,1)} %layer.1) | data formatting | bytes 1048576

commit v5 on v4

--- a/solution.py
+++ b/solution.py
@@ -102,7 +102,7 @@
                 send(n, link).start()
 
     def arrive(n):
-        landed(rbuf.at[pl.ds((n + 1) * TOK, TOK)], r_sem.at[n])
+        landed(rbuf.at[pl.ds(pl.multiple_of((n + 1) * TOK, TOK), TOK)], r_sem.at[n])
 
     def send_x(s, way):
         return pltpu.make_async_remote_copy(
@@ -223,7 +223,7 @@
         def third(u):
             h, b = u % HEADS, u // HEADS
             o = dot(vt[h, :, b * n:(b + 1) * n], ps[u % 2, 0:n, 0:BLK])
-            mix[h * HEAD:(h + 1) * HEAD, b * BLK:(b + 1) * BLK] = o[0:HEAD] / o[HEAD:HEAD + 1]
+            mix[h * HEAD:(h + 1) * HEAD, b * BLK:(b + 1) * BLK] = o[0:HEAD] * (1.0 / o[HEAD:HEAD + 1])
 
         pipeline(4 * HEADS, first, second, third)
 
@@ -249,18 +249,14 @@
     lax.fori_loop(0, 3, single, 0)
 
     def double(r, carry):
-        for k in range(6):
+        arrive(2 * r + 2)
+        arrive(2 * r + 3)
+        for k, sends in ((0, (7, 8, 9)), (1, (10, 11, 12)), (2, (13,)), (4, (14,))):
             @pl.when(r == k)
-            def _(k=k):
-                arrive(2 * k + 2)
-                if k < 3:
-                    start(2 * k + 7)
-                arrive(2 * k + 3)
-                if k < 3:
-                    start(2 * k + 8)
-                else:
-                    start(k + 10)
-                if k in (0, 2, 4):
+            def _(k=k, sends=sends):
+                for n in sends:
+                    start(n)
+                if k % 2 == 0:
                     step_x(k // 2 + 1)
         attend(rbuf[pl.ds(pl.multiple_of((2 * r + 3) * TOK, TOK), 2 * TOK), :])
         return carry
@@ -278,18 +274,25 @@
 
     for h in range(HEADS):
         at = slice(h * HEAD, (h + 1) * HEAD)
-        mix[at, :] = mix[at, :] + acc[h, 0:HEAD] / acc[h, HEAD:HEAD + 1]
+        mix[at, :] = mix[at, :] + acc[h, 0:HEAD] * (1.0 / acc[h, HEAD:HEAD + 1])
     mixed = jnp.transpose(mix[...]).astype(BF16)
     for k in range(3, 6):
         fetch(k).wait()
     resid = (x_ref[...].astype(F32) + dot(mixed, wo[...])).astype(BF16)
     normed_two = rms(resid.astype(F32))
-    total = resid.astype(F32)
-    for k in range(FF // TOK):
-        cols = slice(k * TOK, (k + 1) * TOK)
-        hidden = jax.nn.gelu(dot(normed_two, wup[:, cols])).astype(BF16)
-        total = total + dot(hidden, wdown[cols, :])
-    out_ref[...] = total.astype(BF16)
+    mix[...] = resid.astype(F32)
+
+    def first(k):
+        st[k % 2, 0:TOK] = dot(normed_two, wup[:, k * TOK:(k + 1) * TOK])
+
+    def second(k):
+        ps[k % 2, 0:TOK] = jax.nn.gelu(st[k % 2, 0:TOK]).astype(BF16)
+
+    def third(k):
+        mix[...] += dot(ps[k % 2, 0:TOK], wdown[k * TOK:(k + 1) * TOK, :])
+
+    pipeline(FF // TOK, first, second, third)
+    out_ref[...] = mix[...].astype(out_ref.dtype)
 
 
 def body(features, w_query, w_key, w_value, w_out, w_up, w_down, block_len, cross_blocks, cross_count):

time: 70.4 us -> 70.1 us (level)
  no operation moved by 1% of the time
where the time goes in v5:
time: 70.1 us; the launch traced here: 69.9 us
  Pallas kernels  68.1 us (97%)
  local copies, waits for them, and re-layouts  1.87 us (3%)
    pallas_call x1, Pallas kernels, body(): pl.pallas_call(kernel, out_shape=jax.ShapeDtypeStruct((TOK, D), BF16), in...  68.1 us
    unnamed x1, local copies, waits for them, and re-layouts  1.87 us

profile of v5, /device:TPU:0, one launch (start us, length us, event | category | flops | bytes accessed | tf_op | source)
XLA Modules:
  0.0 69.9 jit_solution(12894799062189009574)
XLA Ops:
  0.0 68.1 %layer.1 = bf16[512,512]{1,0:T(8,128)(2,1)} custom-call(s32[4]{0:T(128)} %len_ref.1, s32[2,4]{1,0:T(2,128)} %bitcast.1, s32[4]{0:T(128)} %count_ref.1, bf16[512,512]{1,0:T(8,128)(2,1)} %x_ref.1, bf16[512,512]{1,0:T(8,128)(2,1)} %wq_hbm.1, bf16[512,512]{1,0:T(8,128)(2,1)} %wk_hbm.1, bf16[512,512]{1,0:T(8,128)(2,1)} %wv_hbm.1, bf16[512,512]{1,0:T(8,128)(2,1)} %wo_hbm.1, ...), custom_call_target="tpu_custom_call" | custom-call | tf_op jit(solution)/shard_map/layer/pallas_call | solution.py:303
  68.1 1.9 %copy.12 = bf16[512,512]{1,0:T(8,128)(2,1)} copy(bf16[512,512]{1,0:T(8,128)(2,1)} %layer.1) | data formatting | bytes 1048576

commit v6 on v5

--- a/solution.py
+++ b/solution.py
@@ -152,13 +152,16 @@
     def keys_of(rows, unused=None):
         n = rows.shape[0]
         ks[0:n, :] = dot(rows, wk[...]).astype(BF16)
-        values = dot_t(wvt[...], rows).astype(BF16)
-        for h in range(HEADS):
-            vt[h, 0:HEAD, 0:n] = values[h * HEAD:(h + 1) * HEAD]
         mask = jnp.where(rows[:, 0:BLK].astype(F32) > FLAG / 2, NEG, 0.0)
         if unused is not None:
             mask = jnp.where(unused, NEG, mask)
         return mask.astype(BF16)
+
+    def values_of(rows):
+        n = rows.shape[0]
+        values = dot_t(wvt[...], rows).astype(BF16)
+        for h in range(HEADS):
+            vt[h, 0:HEAD, 0:n] = values[h * HEAD:(h + 1) * HEAD]
 
     def scores(h, at, n, mask, q):
         lane = lax.broadcasted_iota(jnp.int32, (n, BLK), 1)
@@ -166,9 +169,10 @@
         mine = (lane < HEAD) if h % 2 == 0 else (lane >= HEAD)
         return dot(jnp.where(mine, pair, mask[at:at + n]), q)
 
-    def pipeline(units, first, second, third):
+    def pipeline(units, first, second, third, early=lambda: None):
         first(0)
         first(1)
+        early()
         second(0)
         for u in range(units):
             if u + 1 < units:
@@ -196,7 +200,7 @@
         def third(h):
             acc[h] += dot(vt[h, :, 0:n], ps[h % 2, 0:n])
 
-        pipeline(HEADS, first, second, third)
+        pipeline(HEADS, first, second, third, lambda: values_of(rows))
 
     def cross():
         picked, unused = [], []
@@ -209,7 +213,8 @@
                 picked.append(xbuf[slot])
             at = lax.broadcasted_iota(jnp.int32, (2 * BLK, BLK), 0) // BLK
             unused.append(at >= count_ref[b])
-        mask = keys_of(jnp.concatenate(picked, axis=0), jnp.concatenate(unused, axis=0))
+        rows = jnp.concatenate(picked, axis=0)
+        mask = keys_of(rows, jnp.concatenate(unused, axis=0))
         n = 2 * BLK
 
         def first(u):
@@ -225,7 +230,7 @@
             o = dot(vt[h, :, b * n:(b + 1) * n], ps[u % 2, 0:n, 0:BLK])
             mix[h * HEAD:(h + 1) * HEAD, b * BLK:(b + 1) * BLK] = o[0:HEAD] * (1.0 / o[HEAD:HEAD + 1])
 
-        pipeline(4 * HEADS, first, second, third)
+        pipeline(4 * HEADS, first, second, third, lambda: values_of(rows))
 
     start(1)
 

time: 70.1 us -> 69.8 us (level)
  no operation moved by 1% of the time
where the time goes in v6:
time: 69.8 us; the launch traced here: 69.6 us
  Pallas kernels  67.8 us (97%)
  local copies, waits for them, and re-layouts  1.87 us (3%)
    pallas_call x1, Pallas kernels, body(): pl.pallas_call(kernel, out_shape=jax.ShapeDtypeStruct((TOK, D), BF16), in...  67.8 us
    unnamed x1, local copies, waits for them, and re-layouts  1.87 us

profile of v6, /device:TPU:0, one launch (start us, length us, event | category | flops | bytes accessed | tf_op | source)
XLA Modules:
  0.0 69.6 jit_solution(14435019393252049563)
XLA Ops:
  0.0 67.8 %layer.1 = bf16[512,512]{1,0:T(8,128)(2,1)} custom-call(s32[4]{0:T(128)} %len_ref.1, s32[2,4]{1,0:T(2,128)} %bitcast.1, s32[4]{0:T(128)} %count_ref.1, bf16[512,512]{1,0:T(8,128)(2,1)} %x_ref.1, bf16[512,512]{1,0:T(8,128)(2,1)} %wq_hbm.1, bf16[512,512]{1,0:T(8,128)(2,1)} %wk_hbm.1, bf16[512,512]{1,0:T(8,128)(2,1)} %wv_hbm.1, bf16[512,512]{1,0:T(8,128)(2,1)} %wo_hbm.1, ...), custom_call_target="tpu_custom_call" | custom-call | tf_op jit(solution)/shard_map/layer/pallas_call | solution.py:308
  67.8 1.9 %copy.12 = bf16[512,512]{1,0:T(8,128)(2,1)} copy(bf16[512,512]{1,0:T(8,128)(2,1)} %layer.1) | data formatting | bytes 1048576
